TPU v7x, 32 devices: a whole 2x2x4 slice. The times are simulated.
32 devices in a mesh: leaf: 32 (over z, y, x, core).
Axes of the slice: x: 2, y: 2, z: 4, core: 2. Of those that a mesh axis runs over, the one named last changes fastest.
Arguments:
- right_side: bfloat16 [32768, 256], P('leaf'), may hold values from -6 to 6
- leaf_inv: bfloat16 [32768, 1024], P('leaf'), may hold values from -0.1875 to 0.1875
- right_basis: bfloat16 [4, 32768, 256], P(None, 'leaf'), may hold values from -0.0625 to 0.0625
- left_basis: bfloat16 [4, 32768, 256], P(None, 'leaf'), may hold values from -0.375 to 0.375
- reduced_first: float32 [512, 512], P('leaf'), may hold values from -0.25 to 0.25
- reduced_second: float32 [1024, 512], P('leaf'), may hold values from -0.25 to 0.25
- reduced_third: float32 [2048, 512], P('leaf'), may hold values from -0.25 to 0.25
- reduced_fourth: float32 [4096, 512], P('leaf'), may hold values from -0.25 to 0.25
Outputs:
- solution: float32 [32768, 256], P('leaf')
All inputs are finite; a program needn't handle non-finite values.
Results may differ from a plain program's by a relative error of at most 0.0003.
Values sent between devices are 32-bit elements; how exact they have to be, the bound alone decides.
A program may use at most 64 MiB of HBM per device.

v0:
```python
import jax
import jax.numpy as jnp
from jax import lax
from jax.sharding import PartitionSpec as P

LEVELS = 4


def from_partner(block, axis, bit):
    count = lax.axis_size(axis)
    route = []
    for low in range(count):
        high = low | 1 << bit
        if high != low and high < count:
            route += [(low, high), (high, low)]
    return lax.ppermute(block, axis, route)


def bit_high(position, bitnum):
    return position >> bitnum & 1 == 1


def subtree_sum(partial_value, bit_count):
    totals = partial_value
    for bitnum in range(bit_count):
        totals = totals + from_partner(totals, "leaf", bitnum)
    return totals


def local(
    right_side,
    leaf_inv,
    right_basis,
    left_basis,
    reduced_first,
    reduced_second,
    reduced_third,
    reduced_fourth,
):
    devices_all = lax.axis_size("leaf")
    tree_depth = devices_all.bit_length() - 1
    position = lax.axis_index("leaf")
    reduced_all = (reduced_first, reduced_second, reduced_third, reduced_fourth)
    solution = jnp.dot(leaf_inv, right_side, preferred_element_type=jnp.float32)
    for level in range(LEVELS, 0, -1):
        child_bits = tree_depth - level
        right_rows = right_basis[level - 1].astype(jnp.float32)
        partial_value = lax.dot_general(
            right_rows,
            solution,
            (((0,), (0,)), ((), ())),
            precision=lax.Precision.HIGHEST,
            preferred_element_type=jnp.float32,
        )
        is_upper = bit_high(position, child_bits)
        own_sum = subtree_sum(partial_value, child_bits)
        other_sum = from_partner(own_sum, "leaf", child_bits)
        stacked = jnp.where(
            is_upper,
            jnp.concatenate([other_sum, own_sum], 0),
            jnp.concatenate([own_sum, other_sum], 0),
        )
        gathered = jnp.dot(
            reduced_all[level - 1],
            stacked,
            precision=lax.Precision.HIGHEST,
            preferred_element_type=jnp.float32,
        )
        for bitnum in range(child_bits):
            received = from_partner(gathered, "leaf", bitnum)
            is_high = bit_high(position, bitnum)
            gathered = jnp.where(
                is_high,
                jnp.concatenate([received, gathered], 0),
                jnp.concatenate([gathered, received], 0),
            )
        left_rows = left_basis[level - 1].astype(jnp.float32)
        solution = solution - jnp.dot(
            left_rows, gathered, precision=lax.Precision.HIGHEST, preferred_element_type=jnp.float32
        )
    return solution


def solution(mesh):
    return jax.shard_map(
        local,
        mesh=mesh,
        in_specs=(
            P("leaf", None),
            P("leaf", None),
            P(None, "leaf", None),
            P(None, "leaf", None),
            P("leaf", None),
            P("leaf", None),
            P("leaf", None),
            P("leaf", None),
        ),
        out_specs=P("leaf", None),
        check_vma=False,
    )
```

profile of v0, /device:TPU:0, one launch (start us, length us, event | category | flops | bytes accessed | tf_op | source)
XLA Modules:
  0.0 148.0 jit_solution(17323866203226925790)
XLA Ops:
  4.3 1.9 %convolution_bitcast_fusion.7 = f32[256,256]{1,0:T(8,128)S(1)} fusion(f32[1024,256]{1,0:T(8,128)S(1)} %fusion.76, bf16[4,1024,256]{2,1,0:T(8,128)(2,1)} %param.10), kind=kOutput, calls=%fused_computation.11 | convolution fusion | flops 805306368 | bytes 1835008 | tf_op jit(solution)/shard_map/dot_general | solution.py:48
  7.9 2.9 %collective-permute-start.1 = (f32[256,256]{1,0:T(8,128)S(1)}, f32[256,256]{1,0:T(8,128)S(1)}, u32[]{:S(2)}, u32[]{:S(2)}) collective-permute-start(f32[256,256]{1,0:T(8,128)S(1)} %add.30), channel_id=1, source_target_pairs={{0,2},{2,0},{1,3},{3,1},{4,6},{6,4},{5,7},{7,5},{8,10},{10,8},{9,1... | collective-permute-start | bytes 786440 | tf_op jit(solution)/shard_map/ppermute | solution.py:16
  10.8 6.6 %collective-permute-done.1 = f32[256,256]{1,0:T(8,128)S(1)} collective-permute-done((f32[256,256]{1,0:T(8,128)S(1)}, f32[256,256]{1,0:T(8,128)S(1)}, u32[]{:S(2)}, u32[]{:S(2)}) %collective-permute-start.1) | collective-permute-done | bytes 262176 | tf_op jit(solution)/shard_map/ppermute | solution.py:16
  19.3 2.0 %fusion.3 = f32[1024,256]{1,0:T(8,128)S(1)} fusion(f32[1024,256]{1,0:T(8,128)} %copy-done.3, bf16[4,1024,256]{2,1,0:T(8,128)(2,1)} %param.11, f32[128,256]{1,0:T(8,128)S(1)} %convolution_bitcast_fusion.8, f32[128,256]{1,0:T(8,128)S(1)} %collective-permute-done.2, pred[]{:T(512)S(6)} %eq.10), kind=kOutput, calls=%fused_computation.7 | convolution fusion | flops 805765120 | bytes 2883585 | tf_op jit(solution)/shard_map/dot_general | solution.py:78
  21.4 1.9 %convolution_bitcast_fusion.6 = f32[256,256]{1,0:T(8,128)S(1)} fusion(f32[1024,256]{1,0:T(8,128)S(1)} %fusion.3, bf16[4,1024,256]{2,1,0:T(8,128)(2,1)} %param.10), kind=kOutput, calls=%fused_computation.10 | convolution fusion | flops 805306368 | bytes 1835008 | tf_op jit(solution)/shard_map/dot_general | solution.py:48
  24.9 1.8 %collective-permute-start.4 = (f32[256,256]{1,0:T(8,128)S(1)}, f32[256,256]{1,0:T(8,128)S(1)}, u32[]{:S(2)}, u32[]{:S(2)}) collective-permute-start(f32[256,256]{1,0:T(8,128)S(1)} %add.31), channel_id=1, source_target_pairs={{0,2},{2,0},{1,3},{3,1},{4,6},{6,4},{5,7},{7,5},{8,10},{10,8},{9,1... | collective-permute-start | bytes 786440 | tf_op jit(solution)/shard_map/ppermute | solution.py:16
  26.7 6.6 %collective-permute-done.4 = f32[256,256]{1,0:T(8,128)S(1)} collective-permute-done((f32[256,256]{1,0:T(8,128)S(1)}, f32[256,256]{1,0:T(8,128)S(1)}, u32[]{:S(2)}, u32[]{:S(2)}) %collective-permute-start.4) | collective-permute-done | bytes 262176 | tf_op jit(solution)/shard_map/ppermute | solution.py:16
  33.3 1.8 %collective-permute-start.5 = (f32[256,256]{1,0:T(8,128)S(1)}, f32[256,256]{1,0:T(8,128)}, u32[]{:S(2)}, u32[]{:S(2)}) collective-permute-start(f32[256,256]{1,0:T(8,128)S(1)} %add.32), channel_id=1, source_target_pairs={{0,4},{4,0},{1,5},{5,1},{2,6},{6,2},{3,7},{7,3},{8,12},{12,8},{9,1... | collective-permute-start | bytes 786440 | tf_op jit(solution)/shard_map/ppermute | solution.py:16
  35.2 5.9 %collective-permute-done.5 = f32[256,256]{1,0:T(8,128)} collective-permute-done((f32[256,256]{1,0:T(8,128)S(1)}, f32[256,256]{1,0:T(8,128)}, u32[]{:S(2)}, u32[]{:S(2)}) %collective-permute-start.5) | collective-permute-done | bytes 262176 | tf_op jit(solution)/shard_map/ppermute | solution.py:16
  43.9 1.8 %collective-permute-start.7 = (f32[128,256]{1,0:T(8,128)S(1)}, f32[128,256]{1,0:T(8,128)S(1)}, u32[]{:S(2)}, u32[]{:S(2)}) collective-permute-start(f32[128,256]{1,0:T(8,128)S(1)} %maximum_select_fusion.16), channel_id=1, source_target_pairs={{0,2},{2,0},{1,3},{3,1},{4,6},{6,4},{5,7},{7,5},{8,10},{10,8},{9,1... | collective-permute-start | bytes 393224 | tf_op jit(solution)/shard_map/ppermute | solution.py:16
  45.7 3.9 %collective-permute-done.7 = f32[128,256]{1,0:T(8,128)S(1)} collective-permute-done((f32[128,256]{1,0:T(8,128)S(1)}, f32[128,256]{1,0:T(8,128)S(1)}, u32[]{:S(2)}, u32[]{:S(2)}) %collective-permute-start.7) | collective-permute-done | bytes 131104 | tf_op jit(solution)/shard_map/ppermute | solution.py:16
  51.2 2.2 %convolution_bitcast_fusion.5 = f32[256,256]{1,0:T(8,128)S(1)} fusion(f32[1024,256]{1,0:T(8,128)S(1)} %fusion.2, bf16[4,1024,256]{2,1,0:T(8,128)(2,1)} %param.10), kind=kOutput, calls=%fused_computation.9 | convolution fusion | flops 805306368 | bytes 1835008 | tf_op jit(solution)/shard_map/dot_general | solution.py:48
  56.9 6.6 %collective-permute-done.9 = f32[256,256]{1,0:T(8,128)S(1)} collective-permute-done((f32[256,256]{1,0:T(8,128)S(1)}, f32[256,256]{1,0:T(8,128)S(1)}, u32[]{:S(2)}, u32[]{:S(2)}) %collective-permute-start.9) | collective-permute-done | bytes 262176 | tf_op jit(solution)/shard_map/ppermute | solution.py:16
  63.5 1.8 %collective-permute-start.10 = (f32[256,256]{1,0:T(8,128)S(1)}, f32[256,256]{1,0:T(8,128)S(1)}, u32[]{:S(2)}, u32[]{:S(2)}) collective-permute-start(f32[256,256]{1,0:T(8,128)S(1)} %add.34), channel_id=1, source_target_pairs={{0,4},{4,0},{1,5},{5,1},{2,6},{6,2},{3,7},{7,3},{8,12},{12,8},{9,1... | collective-permute-start | bytes 786440 | tf_op jit(solution)/shard_map/ppermute | solution.py:16
  65.3 5.8 %collective-permute-done.10 = f32[256,256]{1,0:T(8,128)S(1)} collective-permute-done((f32[256,256]{1,0:T(8,128)S(1)}, f32[256,256]{1,0:T(8,128)S(1)}, u32[]{:S(2)}, u32[]{:S(2)}) %collective-permute-start.10) | collective-permute-done | bytes 262176 | tf_op jit(solution)/shard_map/ppermute | solution.py:16
  71.2 1.8 %collective-permute-start.11 = (f32[256,256]{1,0:T(8,128)S(1)}, f32[256,256]{1,0:T(8,128)S(1)}, u32[]{:S(2)}, u32[]{:S(2)}) collective-permute-start(f32[256,256]{1,0:T(8,128)S(1)} %add.35), channel_id=1, source_target_pairs={{0,8},{8,0},{1,9},{9,1},{2,10},{10,2},{3,11},{11,3},{4,12},{12,4},... | collective-permute-start | bytes 786440 | tf_op jit(solution)/shard_map/ppermute | solution.py:16
  73.0 4.9 %collective-permute-done.11 = f32[256,256]{1,0:T(8,128)S(1)} collective-permute-done((f32[256,256]{1,0:T(8,128)S(1)}, f32[256,256]{1,0:T(8,128)S(1)}, u32[]{:S(2)}, u32[]{:S(2)}) %collective-permute-start.11) | collective-permute-done | bytes 262176 | tf_op jit(solution)/shard_map/ppermute | solution.py:16
  81.3 2.6 %collective-permute-done.13 = f32[64,256]{1,0:T(8,128)S(1)} collective-permute-done((f32[64,256]{1,0:T(8,128)S(1)}, f32[64,256]{1,0:T(8,128)S(1)}, u32[]{:S(2)}, u32[]{:S(2)}) %collective-permute-start.13) | collective-permute-done | bytes 65568 | tf_op jit(solution)/shard_map/ppermute | solution.py:16
  83.9 1.8 %collective-permute-start.14 = (f32[128,256]{1,0:T(8,128)S(1)}, f32[128,256]{1,0:T(8,128)S(1)}, u32[]{:S(2)}, u32[]{:S(2)}) collective-permute-start(f32[128,256]{1,0:T(8,128)S(1)} %maximum_select_fusion.17), channel_id=1, source_target_pairs={{0,4},{4,0},{1,5},{5,1},{2,6},{6,2},{3,7},{7,3},{8,12},{12,8},{9,1... | collective-permute-start | bytes 393224 | tf_op jit(solution)/shard_map/ppermute | solution.py:16
  85.7 3.3 %collective-permute-done.14 = f32[128,256]{1,0:T(8,128)S(1)} collective-permute-done((f32[128,256]{1,0:T(8,128)S(1)}, f32[128,256]{1,0:T(8,128)S(1)}, u32[]{:S(2)}, u32[]{:S(2)}) %collective-permute-start.14) | collective-permute-done | bytes 131104 | tf_op jit(solution)/shard_map/ppermute | solution.py:16
  90.6 1.8 %convolution_bitcast_fusion.4 = f32[256,256]{1,0:T(8,128)S(1)} fusion(f32[1024,256]{1,0:T(8,128)S(1)} %fusion.1, bf16[4,1024,256]{2,1,0:T(8,128)(2,1)} %param.10), kind=kOutput, calls=%fused_computation.8 | convolution fusion | flops 805306368 | bytes 1835008 | tf_op jit(solution)/shard_map/dot_general | solution.py:48
  95.8 6.7 %collective-permute-done.16 = f32[256,256]{1,0:T(8,128)S(1)} collective-permute-done((f32[256,256]{1,0:T(8,128)S(1)}, f32[256,256]{1,0:T(8,128)S(1)}, u32[]{:S(2)}, u32[]{:S(2)}) %collective-permute-start.16) | collective-permute-done | bytes 262176 | tf_op jit(solution)/shard_map/ppermute | solution.py:16
  102.6 1.8 %collective-permute-start.17 = (f32[256,256]{1,0:T(8,128)S(1)}, f32[256,256]{1,0:T(8,128)S(1)}, u32[]{:S(2)}, u32[]{:S(2)}) collective-permute-start(f32[256,256]{1,0:T(8,128)S(1)} %add.37), channel_id=1, source_target_pairs={{0,4},{4,0},{1,5},{5,1},{2,6},{6,2},{3,7},{7,3},{8,12},{12,8},{9,1... | collective-permute-start | bytes 786440 | tf_op jit(solution)/shard_map/ppermute | solution.py:16
  104.3 5.8 %collective-permute-done.17 = f32[256,256]{1,0:T(8,128)S(1)} collective-permute-done((f32[256,256]{1,0:T(8,128)S(1)}, f32[256,256]{1,0:T(8,128)S(1)}, u32[]{:S(2)}, u32[]{:S(2)}) %collective-permute-start.17) | collective-permute-done | bytes 262176 | tf_op jit(solution)/shard_map/ppermute | solution.py:16
  110.2 1.8 %collective-permute-start.18 = (f32[256,256]{1,0:T(8,128)S(1)}, f32[256,256]{1,0:T(8,128)S(1)}, u32[]{:S(2)}, u32[]{:S(2)}) collective-permute-start(f32[256,256]{1,0:T(8,128)S(1)} %add.38), channel_id=1, source_target_pairs={{0,8},{8,0},{1,9},{9,1},{2,10},{10,2},{3,11},{11,3},{4,12},{12,4},... | collective-permute-start | bytes 786440 | tf_op jit(solution)/shard_map/ppermute | solution.py:16
  112.0 4.9 %collective-permute-done.18 = f32[256,256]{1,0:T(8,128)S(1)} collective-permute-done((f32[256,256]{1,0:T(8,128)S(1)}, f32[256,256]{1,0:T(8,128)S(1)}, u32[]{:S(2)}, u32[]{:S(2)}) %collective-permute-start.18) | collective-permute-done | bytes 262176 | tf_op jit(solution)/shard_map/ppermute | solution.py:16
  116.9 2.8 %collective-permute-start.19 = (f32[256,256]{1,0:T(8,128)S(1)}, f32[256,256]{1,0:T(8,128)}, u32[]{:S(2)}, u32[]{:S(2)}) collective-permute-start(f32[256,256]{1,0:T(8,128)S(1)} %add.39), channel_id=1, source_target_pairs={{0,16},{16,0},{1,17},{17,1},{2,18},{18,2},{3,19},{19,3},{4,20},{20... | collective-permute-start | bytes 786440 | tf_op jit(solution)/shard_map/ppermute | solution.py:16
  119.7 9.7 %collective-permute-done.19 = f32[256,256]{1,0:T(8,128)} collective-permute-done((f32[256,256]{1,0:T(8,128)S(1)}, f32[256,256]{1,0:T(8,128)}, u32[]{:S(2)}, u32[]{:S(2)}) %collective-permute-start.19) | collective-permute-done | bytes 262176 | tf_op jit(solution)/shard_map/ppermute | solution.py:16
  133.6 2.4 %collective-permute-done.21 = f32[32,256]{1,0:T(8,128)S(1)} collective-permute-done((f32[32,256]{1,0:T(8,128)S(1)}, f32[32,256]{1,0:T(8,128)S(1)}, u32[]{:S(2)}, u32[]{:S(2)}) %collective-permute-start.21) | collective-permute-done | bytes 32800 | tf_op jit(solution)/shard_map/ppermute | solution.py:16
  137.6 2.7 %collective-permute-done.22 = f32[64,256]{1,0:T(8,128)S(1)} collective-permute-done((f32[64,256]{1,0:T(8,128)S(1)}, f32[64,256]{1,0:T(8,128)S(1)}, u32[]{:S(2)}, u32[]{:S(2)}) %collective-permute-start.22) | collective-permute-done | bytes 65568 | tf_op jit(solution)/shard_map/ppermute | solution.py:16
  141.0 4.4 %collective-permute-done.23 = f32[128,256]{1,0:T(8,128)S(1)} collective-permute-done((f32[128,256]{1,0:T(8,128)S(1)}, f32[128,256]{1,0:T(8,128)S(1)}, u32[]{:S(2)}, u32[]{:S(2)}) %collective-permute-start.23) | collective-permute-done | bytes 131104 | tf_op jit(solution)/shard_map/ppermute | solution.py:16
  145.3 2.6 %fusion = f32[1024,256]{1,0:T(8,128)} fusion(f32[1024,256]{1,0:T(8,128)S(1)} %fusion.1, bf16[4,1024,256]{2,1,0:T(8,128)(2,1)} %param.11, f32[128,256]{1,0:T(8,128)S(1)} %maximum_select_fusion.18, f32[128,256]{1,0:T(8,128)S(1)} %collective-permute-done.23, pred[]{:T(512)S(6)} %eq.13), kind=kOutput, calls=%fused_computation.1 | convolution fusion | flops 805765120 | bytes 2883585 | tf_op jit(solution)/shard_map/dot_general | solution.py:78
  (61 shorter events, 32.6 us)
Async XLA Ops:
  0.0 1.6 %copy-start = (bf16[1024,1024]{1,0:T(8,128)(2,1)S(1)}, bf16[1024,1024]{1,0:T(8,128)(2,1)}, u32[]{:S(2)}) copy-start(bf16[1024,1024]{1,0:T(8,128)(2,1)} %param.9) | copy-start | bytes 6291460
  3.4 1.0 copy-start.3
  4.3 13.1 %copy-start.4 = (f32[128,512]{1,0:T(8,128)S(1)}, f32[128,512]{1,0:T(8,128)}, u32[]{:S(2)}) copy-start(f32[128,512]{1,0:T(8,128)} %param.15) | copy-start | bytes 786436
  6.2 1.7 %collective-permute-start = (f32[256,256]{1,0:T(8,128)S(1)}, f32[256,256]{1,0:T(8,128)S(1)}, u32[]{:S(2)}, u32[]{:S(2)}) collective-permute-start(f32[256,256]{1,0:T(8,128)S(1)} %convolution_bitcast_fusion.7), channel_id=1, source_target_pairs={{0,1},{1,0},{2,3},{3,2},{4,5},{5,4},{6,7},{7,6},{8,9},{9,8},{10,11... | collective-permute-start | bytes 786440 | tf_op jit(solution)/shard_map/ppermute | solution.py:16
  7.9 9.5 %collective-permute-start.1 = (f32[256,256]{1,0:T(8,128)S(1)}, f32[256,256]{1,0:T(8,128)S(1)}, u32[]{:S(2)}, u32[]{:S(2)}) collective-permute-start(f32[256,256]{1,0:T(8,128)S(1)} %add.30), channel_id=1, source_target_pairs={{0,2},{2,0},{1,3},{3,1},{4,6},{6,4},{5,7},{7,5},{8,10},{10,8},{9,1... | collective-permute-start | bytes 786440 | tf_op jit(solution)/shard_map/ppermute | solution.py:16
  17.9 1.4 collective-permute-start.2
  21.3 19.7 %copy-start.5 = (f32[64,512]{1,0:T(8,128)S(1)}, f32[64,512]{1,0:T(8,128)}, u32[]{:S(2)}) copy-start(f32[64,512]{1,0:T(8,128)} %param.14) | copy-start | bytes 393220
  23.2 1.6 %collective-permute-start.3 = (f32[256,256]{1,0:T(8,128)S(1)}, f32[256,256]{1,0:T(8,128)S(1)}, u32[]{:S(2)}, u32[]{:S(2)}) collective-permute-start(f32[256,256]{1,0:T(8,128)S(1)} %convolution_bitcast_fusion.6), channel_id=1, source_target_pairs={{0,1},{1,0},{2,3},{3,2},{4,5},{5,4},{6,7},{7,6},{8,9},{9,8},{10,11... | collective-permute-start | bytes 786440 | tf_op jit(solution)/shard_map/ppermute | solution.py:16
  24.9 8.4 %collective-permute-start.4 = (f32[256,256]{1,0:T(8,128)S(1)}, f32[256,256]{1,0:T(8,128)S(1)}, u32[]{:S(2)}, u32[]{:S(2)}) collective-permute-start(f32[256,256]{1,0:T(8,128)S(1)} %add.31), channel_id=1, source_target_pairs={{0,2},{2,0},{1,3},{3,1},{4,6},{6,4},{5,7},{7,5},{8,10},{10,8},{9,1... | collective-permute-start | bytes 786440 | tf_op jit(solution)/shard_map/ppermute | solution.py:16
  33.3 7.7 %collective-permute-start.5 = (f32[256,256]{1,0:T(8,128)S(1)}, f32[256,256]{1,0:T(8,128)}, u32[]{:S(2)}, u32[]{:S(2)}) collective-permute-start(f32[256,256]{1,0:T(8,128)S(1)} %add.32), channel_id=1, source_target_pairs={{0,4},{4,0},{1,5},{5,1},{2,6},{6,2},{3,7},{7,3},{8,12},{12,8},{9,1... | collective-permute-start | bytes 786440 | tf_op jit(solution)/shard_map/ppermute | solution.py:16
  42.6 1.3 collective-permute-start.6
  43.9 5.6 %collective-permute-start.7 = (f32[128,256]{1,0:T(8,128)S(1)}, f32[128,256]{1,0:T(8,128)S(1)}, u32[]{:S(2)}, u32[]{:S(2)}) collective-permute-start(f32[128,256]{1,0:T(8,128)S(1)} %maximum_select_fusion.16), channel_id=1, source_target_pairs={{0,2},{2,0},{1,3},{3,1},{4,6},{6,4},{5,7},{7,5},{8,10},{10,8},{9,1... | collective-permute-start | bytes 393224 | tf_op jit(solution)/shard_map/ppermute | solution.py:16
  51.2 20.0 %copy-start.1 = (f32[1024,256]{1,0:T(8,128)}, f32[1024,256]{1,0:T(8,128)S(1)}, u32[]{:S(2)}) copy-start(f32[1024,256]{1,0:T(8,128)S(1)} %fusion.2) | copy-start | bytes 3145732
  51.2 26.7 %copy-start.6 = (f32[32,512]{1,0:T(8,128)S(1)}, f32[32,512]{1,0:T(8,128)}, u32[]{:S(2)}) copy-start(f32[32,512]{1,0:T(8,128)} %param.13) | copy-start | bytes 196612
  53.4 1.6 %collective-permute-start.8 = (f32[256,256]{1,0:T(8,128)S(1)}, f32[256,256]{1,0:T(8,128)S(1)}, u32[]{:S(2)}, u32[]{:S(2)}) collective-permute-start(f32[256,256]{1,0:T(8,128)S(1)} %convolution_bitcast_fusion.5), channel_id=1, source_target_pairs={{0,1},{1,0},{2,3},{3,2},{4,5},{5,4},{6,7},{7,6},{8,9},{9,8},{10,11... | collective-permute-start | bytes 786440 | tf_op jit(solution)/shard_map/ppermute | solution.py:16
  55.1 8.4 %collective-permute-start.9 = (f32[256,256]{1,0:T(8,128)S(1)}, f32[256,256]{1,0:T(8,128)S(1)}, u32[]{:S(2)}, u32[]{:S(2)}) collective-permute-start(f32[256,256]{1,0:T(8,128)S(1)} %add.33), channel_id=1, source_target_pairs={{0,2},{2,0},{1,3},{3,1},{4,6},{6,4},{5,7},{7,5},{8,10},{10,8},{9,1... | collective-permute-start | bytes 786440 | tf_op jit(solution)/shard_map/ppermute | solution.py:16
  63.5 7.6 %collective-permute-start.10 = (f32[256,256]{1,0:T(8,128)S(1)}, f32[256,256]{1,0:T(8,128)S(1)}, u32[]{:S(2)}, u32[]{:S(2)}) collective-permute-start(f32[256,256]{1,0:T(8,128)S(1)} %add.34), channel_id=1, source_target_pairs={{0,4},{4,0},{1,5},{5,1},{2,6},{6,2},{3,7},{7,3},{8,12},{12,8},{9,1... | collective-permute-start | bytes 786440 | tf_op jit(solution)/shard_map/ppermute | solution.py:16
  71.2 6.7 %collective-permute-start.11 = (f32[256,256]{1,0:T(8,128)S(1)}, f32[256,256]{1,0:T(8,128)S(1)}, u32[]{:S(2)}, u32[]{:S(2)}) collective-permute-start(f32[256,256]{1,0:T(8,128)S(1)} %add.35), channel_id=1, source_target_pairs={{0,8},{8,0},{1,9},{9,1},{2,10},{10,2},{3,11},{11,3},{4,12},{12,4},... | collective-permute-start | bytes 786440 | tf_op jit(solution)/shard_map/ppermute | solution.py:16
  73.0 15.9 %copy-start.2 = (f32[1024,256]{1,0:T(8,128)S(1)}, f32[1024,256]{1,0:T(8,128)}, u32[]{:S(2)}) copy-start(f32[1024,256]{1,0:T(8,128)} %copy-done.1) | copy-start | bytes 3145732
  78.3 1.3 collective-permute-start.12
  79.6 4.3 %collective-permute-start.13 = (f32[64,256]{1,0:T(8,128)S(1)}, f32[64,256]{1,0:T(8,128)S(1)}, u32[]{:S(2)}, u32[]{:S(2)}) collective-permute-start(f32[64,256]{1,0:T(8,128)S(1)} %maximum_select_fusion.19), channel_id=1, source_target_pairs={{0,2},{2,0},{1,3},{3,1},{4,6},{6,4},{5,7},{7,5},{8,10},{10,8},{9,1... | collective-permute-start | bytes 196616 | tf_op jit(solution)/shard_map/ppermute | solution.py:16
  83.9 5.0 %collective-permute-start.14 = (f32[128,256]{1,0:T(8,128)S(1)}, f32[128,256]{1,0:T(8,128)S(1)}, u32[]{:S(2)}, u32[]{:S(2)}) collective-permute-start(f32[128,256]{1,0:T(8,128)S(1)} %maximum_select_fusion.17), channel_id=1, source_target_pairs={{0,4},{4,0},{1,5},{5,1},{2,6},{6,2},{3,7},{7,3},{8,12},{12,8},{9,1... | collective-permute-start | bytes 393224 | tf_op jit(solution)/shard_map/ppermute | solution.py:16
  90.6 38.8 %copy-start.7 = (f32[16,512]{1,0:T(8,128)S(1)}, f32[16,512]{1,0:T(8,128)}, u32[]{:S(2)}) copy-start(f32[16,512]{1,0:T(8,128)} %param.12) | copy-start | bytes 98308
  92.5 1.6 %collective-permute-start.15 = (f32[256,256]{1,0:T(8,128)S(1)}, f32[256,256]{1,0:T(8,128)S(1)}, u32[]{:S(2)}, u32[]{:S(2)}) collective-permute-start(f32[256,256]{1,0:T(8,128)S(1)} %convolution_bitcast_fusion.4), channel_id=1, source_target_pairs={{0,1},{1,0},{2,3},{3,2},{4,5},{5,4},{6,7},{7,6},{8,9},{9,8},{10,11... | collective-permute-start | bytes 786440 | tf_op jit(solution)/shard_map/ppermute | solution.py:16
  94.1 8.4 %collective-permute-start.16 = (f32[256,256]{1,0:T(8,128)S(1)}, f32[256,256]{1,0:T(8,128)S(1)}, u32[]{:S(2)}, u32[]{:S(2)}) collective-permute-start(f32[256,256]{1,0:T(8,128)S(1)} %add.36), channel_id=1, source_target_pairs={{0,2},{2,0},{1,3},{3,1},{4,6},{6,4},{5,7},{7,5},{8,10},{10,8},{9,1... | collective-permute-start | bytes 786440 | tf_op jit(solution)/shard_map/ppermute | solution.py:16
  102.6 7.6 %collective-permute-start.17 = (f32[256,256]{1,0:T(8,128)S(1)}, f32[256,256]{1,0:T(8,128)S(1)}, u32[]{:S(2)}, u32[]{:S(2)}) collective-permute-start(f32[256,256]{1,0:T(8,128)S(1)} %add.37), channel_id=1, source_target_pairs={{0,4},{4,0},{1,5},{5,1},{2,6},{6,2},{3,7},{7,3},{8,12},{12,8},{9,1... | collective-permute-start | bytes 786440 | tf_op jit(solution)/shard_map/ppermute | solution.py:16
  110.2 6.7 %collective-permute-start.18 = (f32[256,256]{1,0:T(8,128)S(1)}, f32[256,256]{1,0:T(8,128)S(1)}, u32[]{:S(2)}, u32[]{:S(2)}) collective-permute-start(f32[256,256]{1,0:T(8,128)S(1)} %add.38), channel_id=1, source_target_pairs={{0,8},{8,0},{1,9},{9,1},{2,10},{10,2},{3,11},{11,3},{4,12},{12,4},... | collective-permute-start | bytes 786440 | tf_op jit(solution)/shard_map/ppermute | solution.py:16
  116.9 12.5 %collective-permute-start.19 = (f32[256,256]{1,0:T(8,128)S(1)}, f32[256,256]{1,0:T(8,128)}, u32[]{:S(2)}, u32[]{:S(2)}) collective-permute-start(f32[256,256]{1,0:T(8,128)S(1)} %add.39), channel_id=1, source_target_pairs={{0,16},{16,0},{1,17},{17,1},{2,18},{18,2},{3,19},{19,3},{4,20},{20... | collective-permute-start | bytes 786440 | tf_op jit(solution)/shard_map/ppermute | solution.py:16
  130.8 1.2 collective-permute-start.20
  132.0 3.9 %collective-permute-start.21 = (f32[32,256]{1,0:T(8,128)S(1)}, f32[32,256]{1,0:T(8,128)S(1)}, u32[]{:S(2)}, u32[]{:S(2)}) collective-permute-start(f32[32,256]{1,0:T(8,128)S(1)} %maximum_select_fusion.21), channel_id=1, source_target_pairs={{0,2},{2,0},{1,3},{3,1},{4,6},{6,4},{5,7},{7,5},{8,10},{10,8},{9,1... | collective-permute-start | bytes 98312 | tf_op jit(solution)/shard_map/ppermute | solution.py:16
  136.0 4.3 %collective-permute-start.22 = (f32[64,256]{1,0:T(8,128)S(1)}, f32[64,256]{1,0:T(8,128)S(1)}, u32[]{:S(2)}, u32[]{:S(2)}) collective-permute-start(f32[64,256]{1,0:T(8,128)S(1)} %maximum_select_fusion.20), channel_id=1, source_target_pairs={{0,4},{4,0},{1,5},{5,1},{2,6},{6,2},{3,7},{7,3},{8,12},{12,8},{9,1... | collective-permute-start | bytes 196616 | tf_op jit(solution)/shard_map/ppermute | solution.py:16
  140.3 5.0 %collective-permute-start.23 = (f32[128,256]{1,0:T(8,128)S(1)}, f32[128,256]{1,0:T(8,128)S(1)}, u32[]{:S(2)}, u32[]{:S(2)}) collective-permute-start(f32[128,256]{1,0:T(8,128)S(1)} %maximum_select_fusion.18), channel_id=1, source_target_pairs={{0,8},{8,0},{1,9},{9,1},{2,10},{10,2},{3,11},{11,3},{4,12},{12,4},... | collective-permute-start | bytes 393224 | tf_op jit(solution)/shard_map/ppermute | solution.py:16
where the time goes:
time: 148 us
  waiting for transfers between devices  93 us (63%)
  starting transfers between devices  30.4 us (21%)
  matrix products  21.2 us (14%)
  local copies, waits for them, and re-layouts  2.59 us (2%)
    ppermute x24, waiting for transfers between devices, from_partner(): return lax.ppermute(block, axis, route)  93 us
    ppermute x24, starting transfers between devices, from_partner(): return lax.ppermute(block, axis, route)  30.4 us
    dot_general x4, matrix products, local(): jnp.dot(left_rows, gathered, precision=lax.Precision.HIGHEST, preferred_e...  7.93 us
    dot_general x4, matrix products, local(): lax.dot_general(right_rows, solution, (((0,), (0,)), ((), ())), precision...  7.8 us
    dot_general x4, matrix products, local(): jnp.dot(reduced_all[level - 1], stacked, precision=lax.Precision.HIGHEST,...  3.7 us
  transfers between devices with their start and end apart: 24, of which 24 were waited for; matrix products, arithmetic and copies ran while one was open for 0% of the time, Pallas kernels for 0%

commit v1 on v0

v1 whole, which is shorter than its diff:
```python
import functools

import jax
import jax.numpy as jnp
from jax import lax
from jax.experimental import pallas as pl
from jax.experimental.pallas import tpu as pltpu
from jax.sharding import PartitionSpec as P

LEVELS = 4
MESH = pl.DeviceIdType.MESH
F32 = jnp.float32
BF16 = jnp.bfloat16
HIGHEST = lax.Precision.HIGHEST
PAIRS = [(j, k) for k in range(LEVELS, 0, -1) for j in range(k - 1, 0, -1)]


def halves(value):
    high = value.astype(BF16)
    return high, (value - high.astype(F32)).astype(BF16)


def flip(position, mask):
    bit, result = 1, position
    while bit <= mask:
        if mask & bit:
            result = result + bit * (1 - 2 * ((position // bit) % 2))
        bit *= 2
    return result


def plan(depth):
    plans = {}
    for level in range(LEVELS, 0, -1):
        sibling = depth - level
        scattered = 2 if sibling - 1 >= 2 else 0
        plans[level] = (sibling, scattered, list(range(1 + scattered, sibling)))
    return plans


def kernel(depth, rank, *refs):
    plans = plan(depth)
    (rhs_h, inv_h, right_h, left_h), reduced_h, out_h = refs[:4], refs[4:8], refs[8]
    it = iter(refs[9:])
    rhs, inv, right, left, x, proj, proj_in = (next(it) for _ in range(7))
    gram, gram_in, own = next(it), next(it), next(it)
    load_sem, out_sem = next(it), next(it)
    core_send, core_recv = next(it), next(it)
    per = {}
    for level in range(LEVELS, 0, -1):
        per[level] = [next(it) for _ in range(12)]
    both = {level: per[level][6] for level in per}

    me = lax.axis_index("leaf")
    core = me % 2
    partner = flip(me, 1)
    leaf, cols = x.shape
    wide = cols // 2

    loads = [
        pltpu.make_async_copy(rhs_h, rhs, load_sem.at[0]),
        pltpu.make_async_copy(inv_h, inv, load_sem.at[1]),
    ]
    for level in range(LEVELS, 0, -1):
        loads.append(pltpu.make_async_copy(right_h.at[level - 1], right.at[level - 1], load_sem.at[2 * level]))
        loads.append(pltpu.make_async_copy(left_h.at[level - 1], left.at[level - 1], load_sem.at[2 * level + 1]))
    base = 2 + 2 * LEVELS
    for level in range(LEVELS, 0, -1):
        loads.append(
            pltpu.make_async_copy(reduced_h[level - 1], per[level][0].at[core], load_sem.at[base + level - 1])
        )
    for copy in loads:
        copy.start()
    right_load = {LEVELS - i: loads[2 + 2 * i] for i in range(LEVELS)}
    left_load = {LEVELS - i: loads[3 + 2 * i] for i in range(LEVELS)}
    reduced_load = {LEVELS - i: loads[base + i] for i in range(LEVELS)}

    top = plans[1][0]
    masks = [1] + [q * 2 for q in range(1, 1 << (top - 1))] + [1 << top]
    barrier = pltpu.get_barrier_semaphore()
    for mask in masks:
        pl.semaphore_signal(barrier, inc=1, device_id=(flip(me, mask),), device_id_type=MESH)

    pending = []

    def send(src, dst, send_sem, recv_sem, target):
        copy = pltpu.make_async_remote_copy(
            src_ref=src, dst_ref=dst, send_sem=send_sem, recv_sem=recv_sem, device_id=(target,), device_id_type=MESH
        )
        copy.start()
        pending.append(copy)
        return copy

    core_count = [0]

    def core_send_to(src, dst):
        i = core_count[0]
        core_count[0] += 1
        return send(src, dst, core_send.at[i], core_recv.at[i], partner)

    loads[0].wait()
    loads[1].wait()
    tile = leaf // 4

    def leaf_step(i, carry):
        rows = pl.ds(pl.multiple_of(i * tile, tile), tile)
        x[rows, :] = jnp.dot(inv[rows, :], rhs[...], preferred_element_type=F32)
        return carry

    lax.fori_loop(0, leaf // tile, leaf_step, 0)
    x_high, x_low = halves(x[...])

    def tdot(a, b):
        return lax.dot_general(a, b, (((0,), (0,)), ((), ())), preferred_element_type=F32)

    proj_copy, gram_copy, reduced_copy, both_copy = {}, {}, {}, {}

    def project(level):
        right_load[level].wait()
        basis = right[level - 1]
        value = tdot(basis, x_high) + tdot(basis, x_low)
        proj[level - 1, 0] = value[:, :wide]
        proj[level - 1, 1] = value[:, wide:]

    def project_send(level):
        proj_copy[level] = core_send_to(proj.at[level - 1, 1 - core], proj_in.at[level - 1])

    def reduced_send(level):
        reduced_load[level].wait()
        kbuf = per[level][0]
        reduced_copy[level] = core_send_to(kbuf.at[core], kbuf.at[core])

    project(LEVELS)
    pl.semaphore_wait(barrier, len(masks))
    project_send(LEVELS)
    reduced_send(LEVELS)

    def prepare():
        for level in range(LEVELS - 1, 0, -1):
            project(level)
            project_send(level)
            for k in range(LEVELS, level, -1):
                if level == LEVELS - 1:
                    left_load[k].wait()
                elif k == level + 1:
                    left_load[k].wait()
                index = PAIRS.index((level, k))
                gram[index] = tdot(right[level - 1], left[k - 1])
                gram_copy[level, k] = core_send_to(gram.at[index], gram_in.at[index])
            reduced_send(level)
        left_load[1].wait()

    def take_proj(level):
        proj_copy[level].wait_recv()
        own[level - 1] = proj[level - 1, core] + proj_in[level - 1]

    def take_gram(level, k):
        gram_copy[level, k].wait_recv()
        index = PAIRS.index((level, k))
        gram_in[index] = gram[index] + gram_in[index]

    def eliminate(level, k):
        index = PAIRS.index((level, k))
        own[level - 1] -= jnp.dot(
            gram_in[index], both[k][core], precision=HIGHEST, preferred_element_type=F32
        )

    def apply(k):
        both_copy[k].wait_recv()
        pieces = [halves(both[k][side]) for side in range(2)]
        high = jnp.concatenate([piece[0] for piece in pieces], 1)
        low = jnp.concatenate([piece[1] for piece in pieces], 1)

        def step(i, carry):
            rows = pl.ds(pl.multiple_of(i * tile, tile), tile)
            w = left[k - 1, rows, :]
            x[rows, :] -= jnp.dot(w, high, preferred_element_type=F32) + jnp.dot(w, low, preferred_element_type=F32)
            return carry

        lax.fori_loop(0, leaf // tile, step, 0)

    def level_step(level, aside):
        kbuf, scatter_in, chain, chain_in, stk, slabs, full = per[level][:7]
        s_send, s_recv, c_sem, g_sem, m_sem = per[level][7:]
        sibling, scattered, butterfly = plans[level]
        parts = 1 << scattered
        size = rank // parts
        place = (me // 2) % parts
        mine = pl.ds(pl.multiple_of(place * size, size), size)
        upper = (me // (1 << sibling)) % 2
        aside = list(aside)

        def beside():
            if aside:
                aside.pop(0)()

        if scattered:
            copies = []
            for q in range(1, parts):
                peer_place = flip(place, q)
                rows = pl.ds(pl.multiple_of(peer_place * size, size), size)
                copies.append(
                    send(own.at[level - 1, rows], scatter_in.at[q], s_send.at[q], s_recv.at[q], flip(me, 2 * q))
                )
            beside()
            total = own[level - 1, mine, :]
            for q, copy in enumerate(copies, 1):
                copy.wait_recv()
                total = total + scatter_in[q]
        else:
            total = own[level - 1]
        for i, bit in enumerate(butterfly):
            chain[i] = total
            copy = send(chain.at[i], chain_in.at[i], c_sem.at[0, i], c_sem.at[1, i], flip(me, 1 << bit))
            beside()
            copy.wait_recv()
            total = total + chain_in[i]
        stk[upper, mine, :] = total
        here = stk.at[upper, mine]
        cross = send(here, here, g_sem.at[0, 0, 0], g_sem.at[1, 0, 0], flip(me, 1 << sibling))
        gathers = []
        for q in range(1, parts):
            gathers.append(send(here, here, g_sem.at[0, 0, q], g_sem.at[1, 0, q], flip(me, 2 * q)))
        beside()
        cross.wait_recv()
        there = stk.at[1 - upper, mine]
        for q in range(1, parts):
            gathers.append(send(there, there, g_sem.at[0, 1, q], g_sem.at[1, 1, q], flip(me, 2 * q)))
        beside()
        reduced_copy[level].wait_recv()
        rows = kbuf.shape[1] * 2
        chip_rows = kbuf[...].reshape(rows, 2 * rank)
        for copy in gathers:
            copy.wait_recv()
        mixed = jnp.dot(
            chip_rows, stk[...].reshape(2 * rank, wide), precision=HIGHEST, preferred_element_type=F32
        )
        chips = 1 << (sibling - 1)
        if chips == 1:
            full[core] = mixed
        else:
            slot = (me // 2) % chips
            slabs[slot] = mixed
            spread = [
                send(slabs.at[slot], slabs.at[slot], m_sem.at[0, q], m_sem.at[1, q], flip(me, 2 * q))
                for q in range(1, chips)
            ]
            while aside:
                beside()
            for copy in spread:
                copy.wait_recv()
            full[core] = slabs[...].reshape(rank, wide)
        while aside:
            beside()
        both_copy[level] = core_send_to(full.at[core], full.at[core])

    take_proj(LEVELS)
    level_step(LEVELS, [prepare])
    for level in range(LEVELS - 1, 0, -1):
        k = level + 1
        if k == LEVELS:
            take_proj(level)
            take_gram(level, k)
        eliminate(level, k)

        def rest(k=k):
            if k == LEVELS:
                for j in range(LEVELS - 2, 0, -1):
                    take_proj(j)
                for j, other in PAIRS:
                    if (j, other) != (LEVELS - 1, LEVELS):
                        take_gram(j, other)
            for j in range(k - 2, 0, -1):
                eliminate(j, k)

        level_step(level, [rest, functools.partial(apply, k)])
    apply(1)
    store = pltpu.make_async_copy(x, out_h, out_sem)
    store.start()
    for copy in pending:
        copy.wait_send()
    store.wait()


def local(right_side, leaf_inv, right_basis, left_basis, *reduced):
    devices = lax.axis_size("leaf")
    depth = devices.bit_length() - 1
    leaf, cols = right_side.shape
    rank = right_basis.shape[2]
    wide = cols // 2
    scratch = [
        pltpu.VMEM(right_side.shape, BF16),
        pltpu.VMEM(leaf_inv.shape, BF16),
        pltpu.VMEM(right_basis.shape, BF16),
        pltpu.VMEM(left_basis.shape, BF16),
        pltpu.VMEM((leaf, cols), F32),
        pltpu.VMEM((LEVELS, 2, rank, wide), F32),
        pltpu.VMEM((LEVELS, rank, wide), F32),
        pltpu.VMEM((len(PAIRS), rank, rank), F32),
        pltpu.VMEM((len(PAIRS), rank, rank), F32),
        pltpu.VMEM((LEVELS, rank, wide), F32),
        pltpu.SemaphoreType.DMA((2 + 3 * LEVELS,)),
        pltpu.SemaphoreType.DMA,
        pltpu.SemaphoreType.DMA((3 * LEVELS + len(PAIRS),)),
        pltpu.SemaphoreType.DMA((3 * LEVELS + len(PAIRS),)),
    ]
    plans = plan(depth)
    for level in range(LEVELS, 0, -1):
        sibling, scattered, butterfly = plans[level]
        parts = 1 << scattered
        steps = max(1, len(butterfly))
        chips = 1 << (sibling - 1)
        rows = reduced[level - 1].shape[0]
        scratch += [
            pltpu.VMEM((2, rows, 2 * rank), F32),
            pltpu.VMEM((parts, rank // parts, wide), F32),
            pltpu.VMEM((steps, rank // parts, wide), F32),
            pltpu.VMEM((steps, rank // parts, wide), F32),
            pltpu.VMEM((2, rank, wide), F32),
            pltpu.VMEM((chips, 2 * rows, wide), F32),
            pltpu.VMEM((2, rank, wide), F32),
            pltpu.SemaphoreType.DMA((parts,)),
            pltpu.SemaphoreType.DMA((parts,)),
            pltpu.SemaphoreType.DMA((2, steps)),
            pltpu.SemaphoreType.DMA((2, 2, parts)),
            pltpu.SemaphoreType.DMA((2, chips)),
        ]
    return pl.pallas_call(
        functools.partial(kernel, depth, rank),
        out_shape=jax.ShapeDtypeStruct((leaf, cols), F32),
        in_specs=[pl.BlockSpec(memory_space=pl.ANY)] * (4 + LEVELS),
        out_specs=pl.BlockSpec(memory_space=pl.ANY),
        scratch_shapes=scratch,
        compiler_params=pltpu.CompilerParams(
            collective_id=0, has_side_effects=True, vmem_limit_bytes=40 * 1024 * 1024
        ),
        name="tree_solve",
    )(right_side, leaf_inv, right_basis, left_basis, *reduced)


def solution(mesh):
    return jax.shard_map(
        local,
        mesh=mesh,
        in_specs=(
            P("leaf", None),
            P("leaf", None),
            P(None, "leaf", None),
            P(None, "leaf", None),
            P("leaf", None),
            P("leaf", None),
            P("leaf", None),
            P("leaf", None),
        ),
        out_specs=P("leaf", None),
        check_vma=False,
    )
```

time: 148 us -> 75 us (0.51)
  waiting for transfers between devices: 93 us -> 0 us
  Pallas kernels: 0 us -> 63.4 us
  starting transfers between devices: 30.4 us -> 0 us
  matrix products: 21.2 us -> 0 us
  local copies, waits for them, and re-layouts: 2.59 us -> 10.2 us
    ppermute x24 -> x0, waiting for transfers between devices: 93 us -> none  [from_partner(): return lax.ppermute(block, axis, route)]
    pallas_call x0 -> x1, Pallas kernels: none -> 63.4 us  [local(): pl.pallas_call(functools.partial(kernel, depth, rank), out_shape=jax.Shap...]
    ppermute x24 -> x0, starting transfers between devices: 30.4 us -> none  [from_partner(): return lax.ppermute(block, axis, route)]
    dot_general x13 -> x0, matrix products: 21.2 us -> none  [the longest x4 7.93 us: local(): jnp.dot(left_rows, gathered, precision=lax.Precision.HIGHEST, preferred_e...]
    unnamed x16 -> x17, local copies, waits for them, and re-layouts: 2.59 us -> 10.2 us
  transfers between devices with their start and end apart: 24 -> 0, of which waited for: 24 -> 0; matrix products, arithmetic and copies ran while one was open for 0% -> 0% of each run, Pallas kernels for 0% -> 0%
where the time goes in v1:
time: 75 us; the launch traced here: 73.7 us
  Pallas kernels  63.4 us (85%)
  local copies, waits for them, and re-layouts  10.2 us (14%)
    pallas_call x1, Pallas kernels, local(): pl.pallas_call(functools.partial(kernel, depth, rank), out_shape=jax.Shap...  63.4 us
    unnamed x17, local copies, waits for them, and re-layouts  10.2 us

profile of v1, /device:TPU:0, one launch (start us, length us, event | category | flops | bytes accessed | tf_op | source)
XLA Modules:
  0.0 73.7 jit_solution(16000068464497420942)
XLA Ops:
  0.0 0.0 copy-start
  0.0 1.6 %copy-done = bf16[1024,1024]{1,0:T(8,128)(2,1)S(1)} copy-done((bf16[1024,1024]{1,0:T(8,128)(2,1)S(1)}, bf16[1024,1024]{1,0:T(8,128)(2,1)}, u32[]{:S(2)}) %copy-start) | copy-done | bytes 2097176
  1.6 0.0 copy-start.1
  1.6 1.6 %copy-done.1 = bf16[4,1024,256]{2,1,0:T(8,128)(2,1)S(1)} copy-done((bf16[4,1024,256]{2,1,0:T(8,128)(2,1)S(1)}, bf16[4,1024,256]{2,1,0:T(8,128)(2,1)}, u32[]{:S(2)}) %copy-start.1) | copy-done | bytes 2097176
  3.2 0.0 copy-start.2
  3.2 1.6 %copy-done.2 = bf16[4,1024,256]{2,1,0:T(8,128)(2,1)S(1)} copy-done((bf16[4,1024,256]{2,1,0:T(8,128)(2,1)S(1)}, bf16[4,1024,256]{2,1,0:T(8,128)(2,1)}, u32[]{:S(2)}) %copy-start.2) | copy-done | bytes 2097176
  4.8 0.0 copy-start.3
  4.8 1.0 %copy-done.3 = bf16[1024,256]{1,0:T(8,128)(2,1)S(1)} copy-done((bf16[1024,256]{1,0:T(8,128)(2,1)S(1)}, bf16[1024,256]{1,0:T(8,128)(2,1)}, u32[]{:S(2)}) %copy-start.3) | copy-done | bytes 524312
  5.8 0.0 copy-start.4
  5.8 0.9 %copy-done.4 = f32[128,512]{1,0:T(8,128)S(1)} copy-done((f32[128,512]{1,0:T(8,128)S(1)}, f32[128,512]{1,0:T(8,128)}, u32[]{:S(2)}) %copy-start.4) | copy-done | bytes 262168
  6.8 0.0 copy-start.5
  6.8 0.9 %copy-done.5 = f32[64,512]{1,0:T(8,128)S(1)} copy-done((f32[64,512]{1,0:T(8,128)S(1)}, f32[64,512]{1,0:T(8,128)}, u32[]{:S(2)}) %copy-start.5) | copy-done | bytes 131096
  7.7 0.0 copy-start.6
  7.7 0.8 %copy-done.6 = f32[32,512]{1,0:T(8,128)S(1)} copy-done((f32[32,512]{1,0:T(8,128)S(1)}, f32[32,512]{1,0:T(8,128)}, u32[]{:S(2)}) %copy-start.6) | copy-done | bytes 65560
  8.5 0.0 copy-start.7
  8.5 0.8 %copy-done.7 = f32[16,512]{1,0:T(8,128)S(1)} copy-done((f32[16,512]{1,0:T(8,128)S(1)}, f32[16,512]{1,0:T(8,128)}, u32[]{:S(2)}) %copy-start.7) | copy-done | bytes 32792
  9.3 63.4 %tree_solve.1 = f32[1024,256]{1,0:T(8,128)S(1)} custom-call(bf16[1024,256]{1,0:T(8,128)(2,1)S(1)} %copy-done.3, bf16[1024,1024]{1,0:T(8,128)(2,1)S(1)} %copy-done, bf16[4,1024,256]{2,1,0:T(8,128)(2,1)S(1)} %copy-done.1, bf16[4,1024,256]{2,1,0:T(8,128)(2,1)S(1)} %copy-done.2, f32[16,512]{1,0:T(8,128)S(1)} %copy-done.7, f32[32,512]{1,0:T(8,128)S(1)} %copy-done.6, ...), custom_call_target="tpu_custom_call" | custom-call | tf_op jit(solution)/shard_map/tree_solve/pallas_call | solution.py:328
  72.7 1.0 %copy.10 = f32[1024,256]{1,0:T(8,128)} copy(f32[1024,256]{1,0:T(8,128)S(1)} %tree_solve.1) | data formatting | bytes 2097152
Async XLA Ops:
  0.0 1.6 %copy-start = (bf16[1024,1024]{1,0:T(8,128)(2,1)S(1)}, bf16[1024,1024]{1,0:T(8,128)(2,1)}, u32[]{:S(2)}) copy-start(bf16[1024,1024]{1,0:T(8,128)(2,1)} %refs_1_.1) | copy-start | bytes 6291460
  1.6 1.6 %copy-start.1 = (bf16[4,1024,256]{2,1,0:T(8,128)(2,1)S(1)}, bf16[4,1024,256]{2,1,0:T(8,128)(2,1)}, u32[]{:S(2)}) copy-start(bf16[4,1024,256]{2,1,0:T(8,128)(2,1)} %refs_2_.1) | copy-start | bytes 6291460
  3.2 1.6 %copy-start.2 = (bf16[4,1024,256]{2,1,0:T(8,128)(2,1)S(1)}, bf16[4,1024,256]{2,1,0:T(8,128)(2,1)}, u32[]{:S(2)}) copy-start(bf16[4,1024,256]{2,1,0:T(8,128)(2,1)} %refs_3_.1) | copy-start | bytes 6291460
  4.8 1.0 %copy-start.3 = (bf16[1024,256]{1,0:T(8,128)(2,1)S(1)}, bf16[1024,256]{1,0:T(8,128)(2,1)}, u32[]{:S(2)}) copy-start(bf16[1024,256]{1,0:T(8,128)(2,1)} %refs_0_.1) | copy-start | bytes 1572868
  5.8 0.9 %copy-start.4 = (f32[128,512]{1,0:T(8,128)S(1)}, f32[128,512]{1,0:T(8,128)}, u32[]{:S(2)}) copy-start(f32[128,512]{1,0:T(8,128)} %refs_7_.1) | copy-start | bytes 786436
  6.8 0.9 %copy-start.5 = (f32[64,512]{1,0:T(8,128)S(1)}, f32[64,512]{1,0:T(8,128)}, u32[]{:S(2)}) copy-start(f32[64,512]{1,0:T(8,128)} %refs_6_.1) | copy-start | bytes 393220
  7.7 0.8 %copy-start.6 = (f32[32,512]{1,0:T(8,128)S(1)}, f32[32,512]{1,0:T(8,128)}, u32[]{:S(2)}) copy-start(f32[32,512]{1,0:T(8,128)} %refs_5_.1) | copy-start | bytes 196612
  8.5 0.8 %copy-start.7 = (f32[16,512]{1,0:T(8,128)S(1)}, f32[16,512]{1,0:T(8,128)}, u32[]{:S(2)}) copy-start(f32[16,512]{1,0:T(8,128)} %refs_4_.1) | copy-start | bytes 98308

commit v2 on v1

--- a/solution.py
+++ b/solution.py
@@ -8,6 +8,7 @@
 from jax.sharding import PartitionSpec as P
 
 LEVELS = 4
+TILES = 4
 MESH = pl.DeviceIdType.MESH
 F32 = jnp.float32
 BF16 = jnp.bfloat16
@@ -48,8 +49,8 @@
     core_send, core_recv = next(it), next(it)
     per = {}
     for level in range(LEVELS, 0, -1):
-        per[level] = [next(it) for _ in range(12)]
-    both = {level: per[level][6] for level in per}
+        per[level] = [next(it) for _ in range(11)]
+    both = {level: per[level][5] for level in per}
 
     me = lax.axis_index("leaf")
     core = me % 2
@@ -57,23 +58,30 @@
     leaf, cols = x.shape
     wide = cols // 2
 
-    loads = [
-        pltpu.make_async_copy(rhs_h, rhs, load_sem.at[0]),
-        pltpu.make_async_copy(inv_h, inv, load_sem.at[1]),
-    ]
+    tile = leaf // TILES
+    slots = {level: (me // 2) % (1 << (plans[level][0] - 1)) for level in plans}
+    loads = [pltpu.make_async_copy(rhs_h, rhs, load_sem.at[0])]
+    for i in range(TILES):
+        rows = pl.ds(i * tile, tile)
+        loads.append(pltpu.make_async_copy(inv_h.at[rows], inv.at[rows], load_sem.at[2 + 3 * LEVELS + i]))
+    inv_load = loads[1:]
+    first = len(loads)
     for level in range(LEVELS, 0, -1):
         loads.append(pltpu.make_async_copy(right_h.at[level - 1], right.at[level - 1], load_sem.at[2 * level]))
         loads.append(pltpu.make_async_copy(left_h.at[level - 1], left.at[level - 1], load_sem.at[2 * level + 1]))
     base = 2 + 2 * LEVELS
     for level in range(LEVELS, 0, -1):
         loads.append(
-            pltpu.make_async_copy(reduced_h[level - 1], per[level][0].at[core], load_sem.at[base + level - 1])
+            pltpu.make_async_copy(
+                reduced_h[level - 1], per[level][0].at[slots[level], core], load_sem.at[base + level - 1]
+            )
         )
-    for copy in loads:
+    right_load = {LEVELS - i: loads[first + 2 * i] for i in range(LEVELS)}
+    left_load = {LEVELS - i: loads[first + 1 + 2 * i] for i in range(LEVELS)}
+    reduced_load = {LEVELS - i: loads[first + 2 * LEVELS + i] for i in range(LEVELS)}
+    early = list(reduced_load.values()) + loads[:first] + [right_load[LEVELS]]
+    for copy in early:
         copy.start()
-    right_load = {LEVELS - i: loads[2 + 2 * i] for i in range(LEVELS)}
-    left_load = {LEVELS - i: loads[3 + 2 * i] for i in range(LEVELS)}
-    reduced_load = {LEVELS - i: loads[base + i] for i in range(LEVELS)}
 
     top = plans[1][0]
     masks = [1] + [q * 2 for q in range(1, 1 << (top - 1))] + [1 << top]
@@ -98,16 +106,38 @@
         core_count[0] += 1
         return send(src, dst, core_send.at[i], core_recv.at[i], partner)
 
+    spread = {}
+
+    def reduced_spread(level):
+        reduced_load[level].wait()
+        kbuf, k_sem = per[level][0], per[level][-1]
+        piece = kbuf.at[slots[level], core]
+        spread[level] = [
+            send(piece, piece, k_sem.at[0, q], k_sem.at[1, q], flip(me, 2 * q)) for q in range(1, kbuf.shape[0])
+        ]
+        spread[level].insert(0, send(piece, piece, k_sem.at[2, 0], k_sem.at[3, 0], partner))
+
+    def reduced_forward(level):
+        kbuf, k_sem = per[level][0], per[level][-1]
+        reduced_copy[level] = [spread[level][0]]
+        for q in range(1, kbuf.shape[0]):
+            spread[level][q].wait_recv()
+            piece = kbuf.at[flip(slots[level], q), core]
+            reduced_copy[level].append(send(piece, piece, k_sem.at[2, q], k_sem.at[3, q], partner))
+
+    pl.semaphore_wait(barrier, len(masks))
+    for level in range(LEVELS, 1, -1):
+        reduced_spread(level)
+
     loads[0].wait()
-    loads[1].wait()
-    tile = leaf // 4
-
-    def leaf_step(i, carry):
-        rows = pl.ds(pl.multiple_of(i * tile, tile), tile)
+    for i in range(TILES):
+        inv_load[i].wait()
+        if i == 0:
+            for copy in loads:
+                if all(copy is not other for other in early):
+                    copy.start()
+        rows = pl.ds(i * tile, tile)
         x[rows, :] = jnp.dot(inv[rows, :], rhs[...], preferred_element_type=F32)
-        return carry
-
-    lax.fori_loop(0, leaf // tile, leaf_step, 0)
     x_high, x_low = halves(x[...])
 
     def tdot(a, b):
@@ -125,15 +155,9 @@
     def project_send(level):
         proj_copy[level] = core_send_to(proj.at[level - 1, 1 - core], proj_in.at[level - 1])
 
-    def reduced_send(level):
-        reduced_load[level].wait()
-        kbuf = per[level][0]
-        reduced_copy[level] = core_send_to(kbuf.at[core], kbuf.at[core])
-
     project(LEVELS)
-    pl.semaphore_wait(barrier, len(masks))
     project_send(LEVELS)
-    reduced_send(LEVELS)
+    reduced_forward(LEVELS)
 
     def prepare():
         for level in range(LEVELS - 1, 0, -1):
@@ -147,7 +171,8 @@
                 index = PAIRS.index((level, k))
                 gram[index] = tdot(right[level - 1], left[k - 1])
                 gram_copy[level, k] = core_send_to(gram.at[index], gram_in.at[index])
-            reduced_send(level)
+            if level == LEVELS - 1:
+                reduced_forward(level)
         left_load[1].wait()
 
     def take_proj(level):
@@ -180,8 +205,8 @@
         lax.fori_loop(0, leaf // tile, step, 0)
 
     def level_step(level, aside):
-        kbuf, scatter_in, chain, chain_in, stk, slabs, full = per[level][:7]
-        s_send, s_recv, c_sem, g_sem, m_sem = per[level][7:]
+        kbuf, scatter_in, chain, chain_in, stk, full = per[level][:6]
+        s_send, s_recv, c_sem, g_sem = per[level][6:10]
         sibling, scattered, butterfly = plans[level]
         parts = 1 << scattered
         size = rank // parts
@@ -209,49 +234,57 @@
                 total = total + scatter_in[q]
         else:
             total = own[level - 1]
-        for i, bit in enumerate(butterfly):
-            chain[i] = total
-            copy = send(chain.at[i], chain_in.at[i], c_sem.at[0, i], c_sem.at[1, i], flip(me, 1 << bit))
+        gathers, crosses = [], []
+        sister = flip(me, 1 << sibling)
+        if not scattered and butterfly:
+            piece = rank // TILES
+            chunks = [pl.ds(i * piece, piece) for i in range(TILES)]
+            sums = [
+                send(
+                    own.at[level - 1, rows],
+                    chain_in.at[0, rows],
+                    c_sem.at[0, i],
+                    c_sem.at[1, i],
+                    flip(me, 1 << butterfly[0]),
+                )
+                for i, rows in enumerate(chunks)
+            ]
             beside()
+            for i, rows in enumerate(chunks):
+                sums[i].wait_recv()
+                stk[upper, rows, :] = own[level - 1, rows, :] + chain_in[0, rows, :]
+                here = stk.at[upper, rows]
+                crosses.append(send(here, here, g_sem.at[0, 0, i], g_sem.at[1, 0, i], sister))
+        else:
+            for i, bit in enumerate(butterfly):
+                chain[i] = total
+                copy = send(chain.at[i], chain_in.at[i], c_sem.at[0, i], c_sem.at[1, i], flip(me, 1 << bit))
+                beside()
+                copy.wait_recv()
+                total = total + chain_in[i]
+            stk[upper, mine, :] = total
+            here = stk.at[upper, mine]
+            crosses.append(send(here, here, g_sem.at[0, 0, 0], g_sem.at[1, 0, 0], sister))
+            for q in range(1, parts):
+                gathers.append(send(here, here, g_sem.at[0, 0, q], g_sem.at[1, 0, q], flip(me, 2 * q)))
+        beside()
+        for copy in crosses:
             copy.wait_recv()
-            total = total + chain_in[i]
-        stk[upper, mine, :] = total
-        here = stk.at[upper, mine]
-        cross = send(here, here, g_sem.at[0, 0, 0], g_sem.at[1, 0, 0], flip(me, 1 << sibling))
-        gathers = []
-        for q in range(1, parts):
-            gathers.append(send(here, here, g_sem.at[0, 0, q], g_sem.at[1, 0, q], flip(me, 2 * q)))
-        beside()
-        cross.wait_recv()
         there = stk.at[1 - upper, mine]
         for q in range(1, parts):
             gathers.append(send(there, there, g_sem.at[0, 1, q], g_sem.at[1, 1, q], flip(me, 2 * q)))
-        beside()
-        reduced_copy[level].wait_recv()
-        rows = kbuf.shape[1] * 2
-        chip_rows = kbuf[...].reshape(rows, 2 * rank)
+        while aside:
+            beside()
+        for copy in reduced_copy[level]:
+            copy.wait_recv()
         for copy in gathers:
             copy.wait_recv()
-        mixed = jnp.dot(
-            chip_rows, stk[...].reshape(2 * rank, wide), precision=HIGHEST, preferred_element_type=F32
+        full[core] = jnp.dot(
+            kbuf[...].reshape(rank, 2 * rank),
+            stk[...].reshape(2 * rank, wide),
+            precision=HIGHEST,
+            preferred_element_type=F32,
         )
-        chips = 1 << (sibling - 1)
-        if chips == 1:
-            full[core] = mixed
-        else:
-            slot = (me // 2) % chips
-            slabs[slot] = mixed
-            spread = [
-                send(slabs.at[slot], slabs.at[slot], m_sem.at[0, q], m_sem.at[1, q], flip(me, 2 * q))
-                for q in range(1, chips)
-            ]
-            while aside:
-                beside()
-            for copy in spread:
-                copy.wait_recv()
-            full[core] = slabs[...].reshape(rank, wide)
-        while aside:
-            beside()
         both_copy[level] = core_send_to(full.at[core], full.at[core])
 
     take_proj(LEVELS)
@@ -263,17 +296,26 @@
             take_gram(level, k)
         eliminate(level, k)
 
-        def rest(k=k):
+        def rest(k=k, level=level):
             if k == LEVELS:
                 for j in range(LEVELS - 2, 0, -1):
                     take_proj(j)
                 for j, other in PAIRS:
                     if (j, other) != (LEVELS - 1, LEVELS):
                         take_gram(j, other)
+            if level == 2:
+                reduced_spread(1)
+            if k == LEVELS:
+                reduced_forward(2)
+
+        def tail(k=k):
             for j in range(k - 2, 0, -1):
                 eliminate(j, k)
-
-        level_step(level, [rest, functools.partial(apply, k)])
+            if k == 2:
+                reduced_forward(1)
+            apply(k)
+
+        level_step(level, [rest, tail])
     apply(1)
     store = pltpu.make_async_copy(x, out_h, out_sem)
     store.start()
@@ -299,10 +341,10 @@
         pltpu.VMEM((len(PAIRS), rank, rank), F32),
         pltpu.VMEM((len(PAIRS), rank, rank), F32),
         pltpu.VMEM((LEVELS, rank, wide), F32),
-        pltpu.SemaphoreType.DMA((2 + 3 * LEVELS,)),
+        pltpu.SemaphoreType.DMA((2 + 3 * LEVELS + TILES,)),
         pltpu.SemaphoreType.DMA,
-        pltpu.SemaphoreType.DMA((3 * LEVELS + len(PAIRS),)),
-        pltpu.SemaphoreType.DMA((3 * LEVELS + len(PAIRS),)),
+        pltpu.SemaphoreType.DMA((2 * LEVELS + len(PAIRS),)),
+        pltpu.SemaphoreType.DMA((2 * LEVELS + len(PAIRS),)),
     ]
     plans = plan(depth)
     for level in range(LEVELS, 0, -1):
@@ -312,27 +354,26 @@
         chips = 1 << (sibling - 1)
         rows = reduced[level - 1].shape[0]
         scratch += [
-            pltpu.VMEM((2, rows, 2 * rank), F32),
+            pltpu.VMEM((chips, 2, rows, 2 * rank), F32),
             pltpu.VMEM((parts, rank // parts, wide), F32),
             pltpu.VMEM((steps, rank // parts, wide), F32),
             pltpu.VMEM((steps, rank // parts, wide), F32),
             pltpu.VMEM((2, rank, wide), F32),
-            pltpu.VMEM((chips, 2 * rows, wide), F32),
             pltpu.VMEM((2, rank, wide), F32),
             pltpu.SemaphoreType.DMA((parts,)),
             pltpu.SemaphoreType.DMA((parts,)),
-            pltpu.SemaphoreType.DMA((2, steps)),
-            pltpu.SemaphoreType.DMA((2, 2, parts)),
-            pltpu.SemaphoreType.DMA((2, chips)),
+            pltpu.SemaphoreType.DMA((2, max(steps, TILES))),
+            pltpu.SemaphoreType.DMA((2, 2, max(parts, TILES))),
+            pltpu.SemaphoreType.DMA((4, chips)),
         ]
     return pl.pallas_call(
         functools.partial(kernel, depth, rank),
         out_shape=jax.ShapeDtypeStruct((leaf, cols), F32),
-        in_specs=[pl.BlockSpec(memory_space=pl.ANY)] * (4 + LEVELS),
+        in_specs=[pl.BlockSpec(memory_space=pltpu.HBM)] * (4 + LEVELS),
         out_specs=pl.BlockSpec(memory_space=pl.ANY),
         scratch_shapes=scratch,
         compiler_params=pltpu.CompilerParams(
-            collective_id=0, has_side_effects=True, vmem_limit_bytes=40 * 1024 * 1024
+            collective_id=0, has_side_effects=True, vmem_limit_bytes=56 * 1024 * 1024
         ),
         name="tree_solve",
     )(right_side, leaf_inv, right_basis, left_basis, *reduced)

time: 75 us -> 59.8 us (0.80)
  local copies, waits for them, and re-layouts: 10.2 us -> 2.26 us
  Pallas kernels: 63.4 us -> 56.5 us
    unnamed x17 -> x1, local copies, waits for them, and re-layouts: 10.2 us -> 2.26 us
    pallas_call x1, Pallas kernels: 63.4 us -> 56.5 us  [local(): pl.pallas_call(functools.partial(kernel, depth, rank), out_shape=jax.Shap...]
where the time goes in v2:
time: 59.8 us; the launch traced here: 58.8 us
  Pallas kernels  56.5 us (94%)
  local copies, waits for them, and re-layouts  2.26 us (4%)
    pallas_call x1, Pallas kernels, local(): pl.pallas_call(functools.partial(kernel, depth, rank), out_shape=jax.Shap...  56.5 us
    unnamed x1, local copies, waits for them, and re-layouts  2.26 us

profile of v2, /device:TPU:0, one launch (start us, length us, event | category | flops | bytes accessed | tf_op | source)
XLA Modules:
  0.0 58.8 jit_solution(13799123830909903766)
XLA Ops:
  0.0 56.5 %tree_solve.1 = f32[1024,256]{1,0:T(8,128)} custom-call(bf16[1024,256]{1,0:T(8,128)(2,1)} %refs_0_.1, bf16[1024,1024]{1,0:T(8,128)(2,1)} %refs_1_.1, bf16[4,1024,256]{2,1,0:T(8,128)(2,1)} %refs_2_.1, bf16[4,1024,256]{2,1,0:T(8,128)(2,1)} %refs_3_.1, f32[16,512]{1,0:T(8,128)} %refs_4_.1, f32[32,512]{1,0:T(8,128)} %refs_5_.1, f32[64,512]{1,0:T(8,128)} %refs_6_.1, ...), custom_call_target="tpu_custom_call" | custom-call | tf_op jit(solution)/shard_map/tree_solve/pallas_call | solution.py:369
  56.5 2.3 %copy.10 = f32[1024,256]{1,0:T(8,128)} copy(f32[1024,256]{1,0:T(8,128)} %tree_solve.1) | data formatting | bytes 2097152

commit v3 on v2

--- a/solution.py
+++ b/solution.py
@@ -12,13 +12,19 @@
 MESH = pl.DeviceIdType.MESH
 F32 = jnp.float32
 BF16 = jnp.bfloat16
-HIGHEST = lax.Precision.HIGHEST
 PAIRS = [(j, k) for k in range(LEVELS, 0, -1) for j in range(k - 1, 0, -1)]
 
 
 def halves(value):
     high = value.astype(BF16)
     return high, (value - high.astype(F32)).astype(BF16)
+
+
+def split_dot(left_parts, value):
+    (high, low), (top, rest) = left_parts, halves(value)
+    wide = value.shape[1]
+    both = jnp.dot(high, jnp.concatenate([top, rest], 1), preferred_element_type=F32)
+    return both[:, :wide] + both[:, wide:] + jnp.dot(low, top, preferred_element_type=F32)
 
 
 def flip(position, mask):
@@ -186,23 +192,23 @@
 
     def eliminate(level, k):
         index = PAIRS.index((level, k))
-        own[level - 1] -= jnp.dot(
-            gram_in[index], both[k][core], precision=HIGHEST, preferred_element_type=F32
-        )
-
-    def apply(k):
+        own[level - 1] -= split_dot(halves(gram_in[index]), both[k][core])
+
+    stores = []
+
+    def apply(k, last=False):
         both_copy[k].wait_recv()
         pieces = [halves(both[k][side]) for side in range(2)]
         high = jnp.concatenate([piece[0] for piece in pieces], 1)
         low = jnp.concatenate([piece[1] for piece in pieces], 1)
 
-        def step(i, carry):
-            rows = pl.ds(pl.multiple_of(i * tile, tile), tile)
+        for i in range(TILES):
+            rows = pl.ds(i * tile, tile)
             w = left[k - 1, rows, :]
             x[rows, :] -= jnp.dot(w, high, preferred_element_type=F32) + jnp.dot(w, low, preferred_element_type=F32)
-            return carry
-
-        lax.fori_loop(0, leaf // tile, step, 0)
+            if last:
+                stores.append(pltpu.make_async_copy(x.at[rows], out_h.at[rows], out_sem.at[i]))
+                stores[-1].start()
 
     def level_step(level, aside):
         kbuf, scatter_in, chain, chain_in, stk, full = per[level][:6]
@@ -277,14 +283,10 @@
             beside()
         for copy in reduced_copy[level]:
             copy.wait_recv()
+        reduced_parts = halves(kbuf[...].reshape(rank, 2 * rank))
         for copy in gathers:
             copy.wait_recv()
-        full[core] = jnp.dot(
-            kbuf[...].reshape(rank, 2 * rank),
-            stk[...].reshape(2 * rank, wide),
-            precision=HIGHEST,
-            preferred_element_type=F32,
-        )
+        full[core] = split_dot(reduced_parts, stk[...].reshape(2 * rank, wide))
         both_copy[level] = core_send_to(full.at[core], full.at[core])
 
     take_proj(LEVELS)
@@ -296,32 +298,32 @@
             take_gram(level, k)
         eliminate(level, k)
 
-        def rest(k=k, level=level):
-            if k == LEVELS:
-                for j in range(LEVELS - 2, 0, -1):
-                    take_proj(j)
-                for j, other in PAIRS:
-                    if (j, other) != (LEVELS - 1, LEVELS):
-                        take_gram(j, other)
+        def rest(level=level):
             if level == 2:
                 reduced_spread(1)
+
+        def tail(k=k):
             if k == LEVELS:
                 reduced_forward(2)
-
-        def tail(k=k):
             for j in range(k - 2, 0, -1):
+                if k == LEVELS:
+                    take_proj(j)
+                    take_gram(j, k)
                 eliminate(j, k)
             if k == 2:
                 reduced_forward(1)
             apply(k)
+            if k == LEVELS:
+                for j, other in PAIRS:
+                    if other < LEVELS:
+                        take_gram(j, other)
 
         level_step(level, [rest, tail])
-    apply(1)
-    store = pltpu.make_async_copy(x, out_h, out_sem)
-    store.start()
+    apply(1, last=True)
     for copy in pending:
         copy.wait_send()
-    store.wait()
+    for copy in stores:
+        copy.wait()
 
 
 def local(right_side, leaf_inv, right_basis, left_basis, *reduced):
@@ -342,7 +344,7 @@
         pltpu.VMEM((len(PAIRS), rank, rank), F32),
         pltpu.VMEM((LEVELS, rank, wide), F32),
         pltpu.SemaphoreType.DMA((2 + 3 * LEVELS + TILES,)),
-        pltpu.SemaphoreType.DMA,
+        pltpu.SemaphoreType.DMA((TILES,)),
         pltpu.SemaphoreType.DMA((2 * LEVELS + len(PAIRS),)),
         pltpu.SemaphoreType.DMA((2 * LEVELS + len(PAIRS),)),
     ]

time: 59.8 us -> 56.6 us (0.946)
  Pallas kernels: 56.5 us -> 53.3 us
    pallas_call x1, Pallas kernels: 56.5 us -> 53.3 us  [local(): pl.pallas_call(functools.partial(kernel, depth, rank), out_shape=jax.Shap...]
where the time goes in v3:
time: 56.6 us; the launch traced here: 55.6 us
  Pallas kernels  53.3 us (94%)
  local copies, waits for them, and re-layouts  2.26 us (4%)
    pallas_call x1, Pallas kernels, local(): pl.pallas_call(functools.partial(kernel, depth, rank), out_shape=jax.Shap...  53.3 us
    unnamed x1, local copies, waits for them, and re-layouts  2.26 us

profile of v3, /device:TPU:0, one launch (start us, length us, event | category | flops | bytes accessed | tf_op | source)
XLA Modules:
  0.0 55.6 jit_solution(10038698697634426979)
XLA Ops:
  0.0 53.3 %tree_solve.1 = f32[1024,256]{1,0:T(8,128)} custom-call(bf16[1024,256]{1,0:T(8,128)(2,1)} %refs_0_.1, bf16[1024,1024]{1,0:T(8,128)(2,1)} %refs_1_.1, bf16[4,1024,256]{2,1,0:T(8,128)(2,1)} %refs_2_.1, bf16[4,1024,256]{2,1,0:T(8,128)(2,1)} %refs_3_.1, f32[16,512]{1,0:T(8,128)} %refs_4_.1, f32[32,512]{1,0:T(8,128)} %refs_5_.1, f32[64,512]{1,0:T(8,128)} %refs_6_.1, ...), custom_call_target="tpu_custom_call" | custom-call | tf_op jit(solution)/shard_map/tree_solve/pallas_call | solution.py:371
  53.3 2.3 %copy.10 = f32[1024,256]{1,0:T(8,128)} copy(f32[1024,256]{1,0:T(8,128)} %tree_solve.1) | data formatting | bytes 2097152
